TPU v7x, 32 devices: a whole 2x2x4 slice. The times are simulated.
32 devices in a mesh: frag: 2 (over x), occ: 4 (over y, core), vir: 4 (over z).
Axes of the slice: x: 2, y: 2, z: 4, core: 2. Of those that a mesh axis runs over, the one named last changes fastest.
Arguments:
- amplitudes: bfloat16 [256, 4096], P(('frag', 'occ')), parts along dimension 0, may hold values from -6 to 6
- panels: bfloat16 [32, 64, 20480], P(('frag', 'occ'), None, 'vir'), parts along dimension 0, may hold values from -0.25 to 0.25
- tile_mask: int32 [32, 320], P(('frag', 'occ'), 'vir'), parts along dimension 0, may hold values 0 or 1
- ranks: int32 [32], P(('frag', 'occ')), parts along dimension 0, may hold values from 16 to 64
- tile_owner: int32 [256], P(('frag', 'occ')), parts along dimension 0, may hold values from 0 to 3, as said below
- tile_row: int32 [256], P(('frag', 'occ')), parts along dimension 0, may hold values from 0 to 3, as said below
- tile_block: int32 [256], P(('frag', 'occ')), parts along dimension 0, may hold values from 0 to 15, as said below
Outputs:
- residual: bfloat16 [32, 64, 20480], P(('frag', 'occ'), None, 'vir'), parts along dimension 0
There are 2 independent parts, one for each index of `frag`. A program takes and returns all parts, laid end to end along the dimension named above; each array names one. Nothing has to cross between parts.
Inputs may be any that keep to these rules, and one draw needn't show every extreme that they name: `tile_owner`: among the 32 tiles of one occ index, one owner drawn per draw is named exactly 8 times by every index, and the other owners share the rest as evenly as possible (counts differ by at most one). No two tiles with the same owner share both tile_row and tile_block. `tile_block`: see tile_row.
All inputs are finite; a program needn't handle non-finite values. No bound on the sum of `tile_mask` on one device may be relied on, other than what follows from the above.
Results may differ from a plain program's by a relative error of at most 0.001.
Values may be sent and summed in bfloat16 or wider, within the bound.
A program may use at most 128 MiB of HBM per device.

v0:
```python
import jax
import jax.numpy as jnp
from jax import lax
from jax.sharding import PartitionSpec as P


def body(amplitudes, panels, tile_mask, ranks, tile_owner, tile_row, tile_block):
    owners = lax.axis_size("occ")
    tile_dev = amplitudes.shape[0]
    tile_width = panels.shape[1]
    columns = panels.shape[2]
    capacity = tile_dev // 4
    row_dev = ranks.shape[0]
    blocks = panels.shape[0] * owners
    slot_count = owners * capacity
    onehot = (tile_owner[:, None] == jnp.arange(owners)[None, :]).astype(jnp.int32)
    before = jnp.sum((jnp.cumsum(onehot, axis=0) - onehot) * onehot, axis=1)
    send_tiles = jnp.zeros((owners, capacity, tile_width * tile_width), amplitudes.dtype)
    send_tiles = send_tiles.at[tile_owner, before].set(amplitudes)
    tile_codes = jnp.stack([tile_row, tile_block + 1], axis=1).astype(jnp.bfloat16)
    send_codes = (
        jnp.zeros((owners, capacity, 2), jnp.bfloat16).at[tile_owner, before].set(tile_codes)
    )
    recv_tiles, recv_codes = (
        lax.all_to_all(send_tiles, "occ", split_axis=0, concat_axis=0, tiled=True),
        lax.all_to_all(send_codes, "occ", split_axis=0, concat_axis=0, tiled=True),
    )
    recv_codes = recv_codes.reshape(slot_count, 2).astype(jnp.int32)
    slot_row = recv_codes[:, 0]
    slot_block = recv_codes[:, 1] - 1
    filled = slot_block >= 0
    row_hot = (slot_row[:, None] == jnp.arange(row_dev)[None, :]) & filled[:, None]
    slot_rank = jnp.sum(row_hot.astype(jnp.int32) * ranks[None, :], axis=1)
    kept_mask = jnp.arange(tile_width)[None, :] < slot_rank[:, None]
    amp_tiles = recv_tiles.reshape(slot_count, tile_width, tile_width)
    amp_tiles = jnp.where(
        kept_mask[:, :, None] & kept_mask[:, None, :], amp_tiles, jnp.zeros_like(amp_tiles)
    )
    col_mask = jnp.repeat(tile_mask, tile_width, axis=1).astype(panels.dtype)
    masked = panels * col_mask[:, None, :]
    cell_index = jnp.where(filled, slot_row * blocks + slot_block, -1)
    picker = (cell_index[:, None] == jnp.arange(row_dev * blocks)[None, :]).astype(jnp.bfloat16)
    pair_block_flat = jnp.einsum(
        "sk,sx->kx",
        picker,
        amp_tiles.reshape(slot_count, tile_width * tile_width),
        preferred_element_type=jnp.float32,
    ).astype(jnp.bfloat16)
    pair_block = (
        pair_block_flat.reshape(row_dev, blocks, tile_width, tile_width)
        .transpose(0, 2, 1, 3)
        .reshape(row_dev * tile_width, blocks * tile_width)
    )
    panel_piece = lax.all_gather(masked, "occ", axis=0, tiled=True)
    count = panel_piece.shape[0]
    running = jnp.dot(
        pair_block,
        panel_piece.reshape(count * tile_width, columns),
        preferred_element_type=jnp.float32,
    )
    running = running.reshape(row_dev, tile_width, columns)
    return running.astype(jnp.bfloat16)


def solution(mesh):
    placed = (
        P(("frag", "occ"), None),
        P(("frag", "occ"), None, "vir"),
        P(("frag", "occ"), "vir"),
        P(("frag", "occ")),
        P(("frag", "occ")),
        P(("frag", "occ")),
        P(("frag", "occ")),
    )
    return jax.shard_map(
        body, mesh=mesh, in_specs=placed, out_specs=P(("frag", "occ"), None, "vir"), check_vma=False
    )
```

profile of v0, /device:TPU:1, one launch (start us, length us, event | category | flops | bytes accessed | tf_op | source)
XLA Modules:
  0.0 101.7 jit_solution(8773936017662841002)
XLA Ops:
  6.5 0.0 all-gather.2.cloned.1.call-start
  6.5 0.7 convert_element_type.33
  7.2 0.1 broadcast_in_dim.15
  7.3 0.1 convert_element_type.34
  7.5 3.4 %broadcast_multiply_fusion = bf16[4,64,5120]{2,1,0:T(8,128)(2,1)} fusion(bf16[4,64,5120]{2,1,0:T(8,128)(2,1)} %param.8, bf16[4,5120]{1,0:T(4,128)(2,1)S(1)} %convert_element_type.34), kind=kLoop, calls=%fused_computation.7 | loop fusion | flops 1310720 | bytes 5283840 | tf_op jit(solution)/shard_map/mul | solution.py:40
  10.9 0.0 all-gather.2.cloned.1.call-update
  10.9 0.6 copy-done.2
  11.5 0.0 copy-done.3
  11.6 0.1 copy.13
  11.7 0.0 copy-done.1
  11.7 0.1 fusion.10
  11.7 0.1 reduce_window_sum.11
  11.8 0.2 select_reduce_fusion.1
  12.0 2.1 %scatter_fusion = bf16[4,8,2]{2,1,0:T(8,128)(2,1)S(1)} fusion(bf16[4,8,2]{2,1,0:T(8,128)(2,1)S(1)} %broadcast_in_dim.11, s32[32]{0:T(128)S(1)} %fusion.16, bf16[32,2]{1,0:T(8,128)(2,1)S(1)} %copy.13), kind=kCustom, calls=%fused_computation | custom fusion | bytes 640 | tf_op jit(solution)/shard_map/scatter | solution.py:22
  14.2 0.6 copy.14
  14.8 4.3 %all-to-all-start = ((bf16[4,8,2]{1,2,0:T(2,128)(2,1)}), bf16[4,8,2]{1,2,0:T(2,128)(2,1)S(1)}, u32[]{:S(2)}, u32[]{:S(2)}) async-start(bf16[4,8,2]{1,2,0:T(2,128)(2,1)} %copy.14), calls=%async_computation | async-start | bytes 4096 | tf_op jit(solution)/shard_map/all_to_all | solution.py:26
  19.1 0.7 broadcast_in_dim.13
  19.8 0.0 copy-done
  19.8 9.3 %scatter_fusion.1 = bf16[4,8,4096]{2,1,0:T(8,128)(2,1)} fusion(bf16[4,8,4096]{2,1,0:T(8,128)(2,1)} %broadcast_in_dim.13, s32[32]{0:T(128)S(1)} %fusion.16, bf16[32,4096]{1,0:T(8,128)(2,1)S(1)} %copy-done), kind=kCustom, calls=%fused_computation.1 | custom fusion | bytes 786688 | tf_op jit(solution)/shard_map/scatter | solution.py:19
  29.1 0.0 all-to-all-done
  29.1 3.4 %all-to-all-start.1 = ((bf16[4,8,4096]{2,1,0:T(8,128)(2,1)}), bf16[4,8,4096]{2,1,0:T(8,128)(2,1)S(1)}, u32[]{:S(2)}, u32[]{:S(2)}) async-start(bf16[4,8,4096]{2,1,0:T(8,128)(2,1)} %scatter_fusion.1), calls=%async_computation.1 | async-start | bytes 524288 | tf_op jit(solution)/shard_map/all_to_all | solution.py:25
  32.5 0.1 reshape.79
  32.6 0.0 copy-done.4
  32.6 0.2 select_reduce_fusion
  32.8 0.1 iota_compare_fusion.1
  32.9 0.3 broadcast_and_fusion
  33.2 0.7 and.33
  34.0 6.9 %all-to-all-done.1 = bf16[4,8,4096]{2,1,0:T(8,128)(2,1)S(1)} async-done(((bf16[4,8,4096]{2,1,0:T(8,128)(2,1)}), bf16[4,8,4096]{2,1,0:T(8,128)(2,1)S(1)}, u32[]{:S(2)}, u32[]{:S(2)}) %all-to-all-start.1) | async-done | bytes 262176 | tf_op jit(solution)/shard_map/all_to_all | solution.py:25
  40.9 0.4 convolution_convert_fusion
  41.3 1.1 %reshape.78 = bf16[4,16,64,64]{3,2,1,0:T(8,128)(2,1)S(1)} reshape(bf16[64,4096]{1,0:T(8,128)(2,1)S(1)} %convolution_convert_fusion) | data formatting | bytes 1048576 | tf_op jit(solution)/shard_map/reshape | solution.py:50
  42.4 44.2 %all-gather.2.cloned.1.call-done = bf16[16,64,5120]{2,1,0:T(8,128)(2,1)} async-done(((bf16[4,64,5120]{2,1,0:T(8,128)(2,1)}), bf16[16,64,5120]{2,1,0:T(8,128)(2,1)}) %all-gather.2.cloned.1.call-update) | async-done | bytes 10485776 | tf_op jit(solution)/shard_map/all_gather | solution.py:54
  86.6 8.2 %fusion.5 = bf16[4,64,5120]{2,1,0:T(8,128)(2,1)} fusion(bf16[16,64,5120]{2,1,0:T(8,128)(2,1)} %all-gather.2.cloned.1.call-done, bf16[4,16,64,64]{3,2,1,0:T(8,128)(2,1)S(1)} %reshape.78), kind=kOutput, calls=%fused_computation.5 | convolution fusion | flops 2685665280 | bytes 13631488 | tf_op jit(solution)/shard_map/dot_general | solution.py:56
  (12 shorter events, 0.1 us)
Async XLA Ops:
  6.5 80.0 %all-gather.2.cloned.1.call-start = ((), (), s32[]{:S(2)}) async-start(), calls=%async_computation.2 | async-start | bytes 13107200 | tf_op jit(solution)/shard_map/all_gather | solution.py:54
  10.9 0.7 copy-start.2
  10.9 0.7 copy-start.3
  10.9 0.8 copy-start.1
  10.9 8.9 %copy-start = (bf16[32,4096]{1,0:T(8,128)(2,1)S(1)}, bf16[32,4096]{1,0:T(8,128)(2,1)}, u32[]{:S(2)}) copy-start(bf16[32,4096]{1,0:T(8,128)(2,1)} %param.7) | copy-start | bytes 786436
  14.8 14.3 %all-to-all-start = ((bf16[4,8,2]{1,2,0:T(2,128)(2,1)}), bf16[4,8,2]{1,2,0:T(2,128)(2,1)S(1)}, u32[]{:S(2)}, u32[]{:S(2)}) async-start(bf16[4,8,2]{1,2,0:T(2,128)(2,1)} %copy.14), calls=%async_computation | async-start | bytes 4096 | tf_op jit(solution)/shard_map/all_to_all | solution.py:26
  19.1 13.5 %copy-start.4 = (s32[4]{0:T(128)S(1)}, s32[4]{0:T(128)}, u32[]{:S(2)}) copy-start(s32[4]{0:T(128)} %param.10) | copy-start | bytes 52
  29.1 11.8 %all-to-all-start.1 = ((bf16[4,8,4096]{2,1,0:T(8,128)(2,1)}), bf16[4,8,4096]{2,1,0:T(8,128)(2,1)S(1)}, u32[]{:S(2)}, u32[]{:S(2)}) async-start(bf16[4,8,4096]{2,1,0:T(8,128)(2,1)} %scatter_fusion.1), calls=%async_computation.1 | async-start | bytes 524288 | tf_op jit(solution)/shard_map/all_to_all | solution.py:25
Sparse Core Ops, SparseCore 0:
  11.0 75.5 all-gather.1
where the time goes:
time: 102 us
  waiting for transfers between devices  51.1 us (50%)
  local copies, waits for them, and re-layouts  15.7 us (15%)
  between operations  13.5 us (13%)
  matrix products  8.64 us (8%)
  starting transfers between devices  7.68 us (8%)
  other arithmetic  5.08 us (5%)
    all_gather x1, waiting for transfers between devices, body(): panel_piece = lax.all_gather(masked, 'occ', axis=0, tiled=True)  44.2 us
    scatter x1, local copies, waits for them, and re-layouts, body(): send_tiles = send_tiles.at[tile_owner, before].set(amplitudes)  9.27 us
    dot_general x1, matrix products, body(): jnp.dot(pair_block, panel_piece.reshape(count * tile_width, columns), pre...  8.23 us
    all_to_all x1, waiting for transfers between devices, body(): lax.all_to_all(send_tiles, 'occ', split_axis=0, concat_axis=0, tiled=True)  6.91 us
    all_to_all x1, starting transfers between devices, body(): lax.all_to_all(send_codes, 'occ', split_axis=0, concat_axis=0, tiled=True)  4.29 us
    mul x1, other arithmetic, body(): masked = panels * col_mask[:, None, :]  3.43 us
    all_to_all x1, starting transfers between devices, body(): lax.all_to_all(send_tiles, 'occ', split_axis=0, concat_axis=0, tiled=True)  3.39 us
    scatter x2, local copies, waits for them, and re-layouts, body(): jnp.zeros((owners, capacity, 2), jnp.bfloat16).at[tile_owner, before]  2.77 us
  transfers between devices with their start and end apart: 3, of which 2 were waited for; matrix products, arithmetic and copies ran while one was open for 16% of the time, Pallas kernels for 0%

commit v1 on v0

v1 whole, which is shorter than its diff:
```python
import functools

import jax
import jax.numpy as jnp
from jax import lax
from jax.experimental import pallas as pl
from jax.experimental.pallas import tpu as pltpu
from jax.sharding import PartitionSpec as P

MESH = pl.DeviceIdType.MESH
CHUNK = 512
EARLY = 2


def kernel(
    n, row_dev, width, capacity,
    panel_hbm, amp_hbm, mask_ref, rank_ref, owner_ref, row_ref, block_ref,
    out_hbm,
    gathered, amp, outbox, inbox, code_out, code_in, cells_s, block_f32, block_bf, staged,
    load_sem, amp_sem, far_send, far_recv, mate_send, mate_recv, fwd_send, fwd_recv,
    box_send, box_recv, code_send, code_recv, out_sem,
):
    me = lax.axis_index("occ")
    ranks_of_chips = n // 2
    mate = me + 1 - 2 * lax.rem(me, 2)
    chunks = gathered.shape[0]
    depth = panel_hbm.shape[0]
    local_blocks = depth // width
    blocks = local_blocks * n
    tiles = amp.shape[0]
    flat = amp.shape[1]
    half = flat // 2
    cells = row_dev * blocks

    def peer(distance):
        return lax.rem(me + distance, n)

    def slot(k, source):
        return gathered.at[k, pl.ds(pl.multiple_of(source * depth, depth), depth), :]

    def columns(k):
        return pl.ds(pl.multiple_of(k * CHUNK, CHUNK), CHUNK)

    def load(k):
        return pltpu.make_async_copy(panel_hbm.at[:, columns(k)], slot(k, me), load_sem.at[k])

    def far(k, d):
        return pltpu.make_async_remote_copy(
            src_ref=slot(k, me), dst_ref=slot(k, me),
            send_sem=far_send.at[d - 1, k], recv_sem=far_recv.at[d - 1, k],
            device_id={"occ": peer(2 * d)}, device_id_type=MESH,
        )

    def near(k):
        return pltpu.make_async_remote_copy(
            src_ref=slot(k, me), dst_ref=slot(k, me),
            send_sem=mate_send.at[k], recv_sem=mate_recv.at[k],
            device_id={"occ": mate}, device_id_type=MESH,
        )

    def forward(k, d):
        source = peer(n - 2 * d)
        return pltpu.make_async_remote_copy(
            src_ref=slot(k, source), dst_ref=slot(k, source),
            send_sem=fwd_send.at[d - 1, k], recv_sem=fwd_recv.at[d - 1, k],
            device_id={"occ": mate}, device_id_type=MESH,
        )

    def box(d):
        target = peer(d)
        return pltpu.make_async_remote_copy(
            src_ref=outbox.at[target], dst_ref=inbox.at[me],
            send_sem=box_send.at[d - 1], recv_sem=box_recv.at[d - 1],
            device_id={"occ": target}, device_id_type=MESH,
        )

    def code(d):
        target = peer(d)
        return pltpu.make_async_remote_copy(
            src_ref=code_out.at[target], dst_ref=code_in.at[me],
            send_sem=code_send.at[d - 1], recv_sem=code_recv.at[d - 1],
            device_id={"occ": target}, device_id_type=MESH,
        )

    @pl.loop(0, chunks)
    def _(k):
        load(k).start()

    fetch_amp = pltpu.make_async_copy(amp_hbm, amp, amp_sem)
    fetch_amp.start()

    barrier = pltpu.get_barrier_semaphore()
    for d in range(1, n):
        pl.semaphore_signal(barrier, inc=1, device_id={"occ": peer(d)}, device_id_type=MESH)
    pl.semaphore_wait(barrier, n - 1)

    col_tiles = mask_ref.shape[1]

    def send_chunk(k):
        tile_of = (k * CHUNK + lax.broadcasted_iota(jnp.int32, (col_tiles, CHUNK), 1)) // width
        spread = (tile_of == lax.broadcasted_iota(jnp.int32, (col_tiles, CHUNK), 0))
        kept = jnp.dot(
            mask_ref[...].astype(jnp.float32).astype(jnp.bfloat16),
            spread.astype(jnp.float32).astype(jnp.bfloat16),
            preferred_element_type=jnp.float32,
        ).astype(jnp.bfloat16)
        load(k).wait()
        for b in range(local_blocks):
            rows = pl.ds(pl.multiple_of(me * depth + b * width, width), width)
            gathered[k, rows, :] = gathered[k, rows, :] * kept[b : b + 1, :]
        for d in range(1, ranks_of_chips):
            far(k, d).start()
        near(k).start()

    early = min(EARLY, chunks)

    @pl.loop(0, early)
    def _(k):
        send_chunk(k)

    owner = owner_ref[...]
    tile_lane = lax.broadcasted_iota(jnp.int32, (tiles, tiles), 1)
    tile_sub = lax.broadcasted_iota(jnp.int32, (tiles, tiles), 0)
    owner_col = jnp.sum(
        jnp.where(tile_lane == tile_sub, jnp.broadcast_to(owner, (tiles, tiles)), 0),
        axis=1, keepdims=True,
    )
    same = (owner_col == owner) & (tile_sub < tile_lane)
    before = jnp.sum(same.astype(jnp.int32), axis=0, keepdims=True)
    tile_code = row_ref[...] * blocks + block_ref[...] + 1
    fetch_amp.wait()
    slot_sub = lax.rem(lax.broadcasted_iota(jnp.int32, (2 * capacity, tiles), 0), capacity)
    for o in range(n):
        chosen = (owner == o) & (before == slot_sub)
        picked = jnp.dot(
            chosen[:capacity].astype(jnp.float32).astype(jnp.bfloat16), amp[...],
            preferred_element_type=jnp.float32,
        )
        outbox[o] = jnp.concatenate([picked[:, :half], picked[:, half:]], axis=0).astype(jnp.bfloat16)
        code_col = jnp.sum(jnp.where(chosen, tile_code, 0), axis=1, keepdims=True)
        lane = lax.broadcasted_iota(jnp.int32, (2 * capacity, 128), 1)
        sub = lax.broadcasted_iota(jnp.int32, (2 * capacity, 128), 0)
        code_row = jnp.sum(jnp.where(lane == sub, code_col, 0), axis=0, keepdims=True)
        code_out[o] = jnp.broadcast_to(code_row, (8, 128))
    for d in range(1, n):
        box(d).start()
        code(d).start()

    @pl.loop(early, chunks)
    def _(k):
        send_chunk(k)

    inbox[me] = outbox[me]
    code_in[me] = code_out[me]
    for d in range(1, n):
        box(d).wait()
        code(d).wait()

    cell_sub = lax.broadcasted_iota(jnp.int32, (cells, 2 * capacity), 0)
    slot_half = lax.broadcasted_iota(jnp.int32, (cells, 2 * capacity), 1) // capacity
    ranks = rank_ref[...]
    rank_lane = lax.broadcasted_iota(jnp.int32, (cells, row_dev), 1)
    cell_row = lax.broadcasted_iota(jnp.int32, (cells, row_dev), 0) // blocks
    cell_rank = jnp.sum(jnp.where(rank_lane == cell_row, ranks, 0), axis=1, keepdims=True)
    per_half = half // 128

    for h in range(2):
        total = jnp.zeros((cells, half), jnp.float32)
        for o in range(n):
            here = (code_in[o][0:1, : 2 * capacity] == cell_sub + 1) & (slot_half == h)
            total = total + jnp.dot(
                here.astype(jnp.float32).astype(jnp.bfloat16), inbox[o],
                preferred_element_type=jnp.float32,
            )
        place = h * half + lax.broadcasted_iota(jnp.int32, (cells, half), 1)
        kept = (place // width < cell_rank) & (lax.rem(place, width) < cell_rank)
        total = jnp.where(kept, total, 0.0)
        for r in range(per_half):
            start = (h * per_half + r) * cells
            cells_s[start : start + cells, :] = total[:, r * 128 : (r + 1) * 128]

    pairs = width // 2
    low = lax.broadcasted_iota(jnp.int32, (pairs, 128), 1) < width
    for row in range(row_dev):
        @pl.loop(0, blocks // 2)
        def _(q):
            first = cells_s[pl.ds(row * blocks + 2 * q, pairs, stride=cells), :]
            second = cells_s[pl.ds(row * blocks + 2 * q + 1, pairs, stride=cells), :]
            even = jnp.where(low, first, pltpu.roll(second, width, 1))
            odd = jnp.where(low, pltpu.roll(first, width, 1), second)
            block_f32[q, pl.ds(row * width, pairs, stride=2), :] = even
            block_f32[q, pl.ds(row * width + 1, pairs, stride=2), :] = odd

    for q in range(blocks // 2):
        block_bf[:, q * 128 : (q + 1) * 128] = block_f32[q].astype(jnp.bfloat16)

    def store(k):
        return pltpu.make_async_copy(staged.at[k], out_hbm.at[:, columns(k)], out_sem.at[k])

    def multiply(k):
        near(k).wait_recv()
        for d in range(1, ranks_of_chips):
            forward(k, d).wait_recv()
        staged[k] = jnp.dot(
            block_bf[...], gathered[k], preferred_element_type=jnp.float32
        ).astype(jnp.bfloat16)
        store(k).start()

    def pass_on(k):
        for d in range(1, ranks_of_chips):
            far(k, d).wait_recv()
            forward(k, d).start()

    pass_on(0)

    @pl.loop(1, chunks)
    def _(k):
        pass_on(k)
        multiply(k - 1)

    multiply(chunks - 1)

    @pl.loop(0, chunks)
    def _(k):
        near(k).wait_send()
        for d in range(1, ranks_of_chips):
            far(k, d).wait_send()
            forward(k, d).wait_send()
        store(k).wait()


def body(amplitudes, panels, tile_mask, ranks, tile_owner, tile_row, tile_block):
    n = lax.axis_size("occ")
    tiles, flat = amplitudes.shape
    local_blocks, width, cols = panels.shape
    row_dev = ranks.shape[0]
    capacity = tiles // 4
    blocks = local_blocks * n
    depth = local_blocks * width
    chunks = cols // CHUNK
    others = n - 1
    chips = n // 2
    cells = row_dev * blocks
    whole = pl.BlockSpec(memory_space=pl.ANY)
    vmem = pl.BlockSpec(memory_space=pltpu.VMEM)
    dma = pltpu.SemaphoreType.DMA
    out = pl.pallas_call(
        functools.partial(kernel, n, row_dev, width, capacity),
        out_shape=jax.ShapeDtypeStruct((row_dev * width, cols), jnp.bfloat16),
        in_specs=[whole, whole] + [vmem] * 5,
        out_specs=whole,
        scratch_shapes=[
            pltpu.VMEM((chunks, blocks * width, CHUNK), jnp.bfloat16),
            pltpu.VMEM((tiles, flat), jnp.bfloat16),
            pltpu.VMEM((n, 2 * capacity, flat // 2), jnp.bfloat16),
            pltpu.VMEM((n, 2 * capacity, flat // 2), jnp.bfloat16),
            pltpu.VMEM((n, 8, 128), jnp.int32),
            pltpu.VMEM((n, 8, 128), jnp.int32),
            pltpu.VMEM((flat // 128 * cells, 128), jnp.float32),
            pltpu.VMEM((blocks // 2, row_dev * width, 128), jnp.float32),
            pltpu.VMEM((row_dev * width, blocks * width), jnp.bfloat16),
            pltpu.VMEM((chunks, row_dev * width, CHUNK), jnp.bfloat16),
            dma((chunks,)), dma,
            dma((chips - 1, chunks)), dma((chips - 1, chunks)),
            dma((chunks,)), dma((chunks,)),
            dma((chips - 1, chunks)), dma((chips - 1, chunks)),
            dma((others,)), dma((others,)), dma((others,)), dma((others,)),
            dma((chunks,)),
        ],
        compiler_params=pltpu.CompilerParams(
            collective_id=0, has_side_effects=True, vmem_limit_bytes=56 * 1024 * 1024
        ),
    )(
        panels.reshape(depth, cols), amplitudes, tile_mask, ranks[None], tile_owner[None],
        tile_row[None], tile_block[None],
    )
    return out.reshape(row_dev, width, cols)


def solution(mesh):
    placed = (
        P(("frag", "occ"), None),
        P(("frag", "occ"), None, "vir"),
        P(("frag", "occ"), "vir"),
        P(("frag", "occ")),
        P(("frag", "occ")),
        P(("frag", "occ")),
        P(("frag", "occ")),
    )
    return jax.shard_map(
        body, mesh=mesh, in_specs=placed, out_specs=P(("frag", "occ"), None, "vir"), check_vma=False
    )
```

time: 102 us -> 71.2 us (0.70)
  Pallas kernels: 0 us -> 67.6 us
  waiting for transfers between devices: 51.1 us -> 0 us
  between operations: 13.5 us -> 0.01 us
  local copies, waits for them, and re-layouts: 15.7 us -> 3.4 us
  matrix products: 8.64 us -> 0 us
  starting transfers between devices: 7.68 us -> 0 us
  other arithmetic: 5.08 us -> 0 us
    pallas_call x0 -> x1, Pallas kernels: none -> 67.6 us  [body(): pl.pallas_call(functools.partial(kernel, n, row_dev, width, capacity), ou...]
    all_gather x1 -> x0, waiting for transfers between devices: 44.2 us -> none  [body(): panel_piece = lax.all_gather(masked, 'occ', axis=0, tiled=True)]
    scatter x3 -> x0, local copies, waits for them, and re-layouts: 12 us -> none  [the longest x1 9.27 us: body(): send_tiles = send_tiles.at[tile_owner, before].set(amplitudes)]
    dot_general x2 -> x0, matrix products: 8.64 us -> none  [the longest x1 8.23 us: body(): jnp.dot(pair_block, panel_piece.reshape(count * tile_width, columns), pre...]
    all_to_all x2 -> x0, starting transfers between devices: 7.68 us -> none  [the longest x1 4.29 us: body(): lax.all_to_all(send_codes, 'occ', split_axis=0, concat_axis=0, tiled=True)]
    all_to_all x2 -> x0, waiting for transfers between devices: 6.91 us -> none  [the longest x1 6.91 us: body(): lax.all_to_all(send_tiles, 'occ', split_axis=0, concat_axis=0, tiled=True)]
    mul x1 -> x0, other arithmetic: 3.43 us -> none  [body(): masked = panels * col_mask[:, None, :]]
    unnamed x10 -> x1, local copies, waits for them, and re-layouts: 0.65 us -> 3.4 us
  transfers between devices with their start and end apart: 3 -> 0, of which waited for: 2 -> 0; matrix products, arithmetic and copies ran while one was open for 16% -> 0% of each run, Pallas kernels for 0% -> 0%
where the time goes in v1:
time: 71.2 us; the launch traced here: 71 us
  Pallas kernels  67.6 us (95%)
  local copies, waits for them, and re-layouts  3.4 us (5%)
    pallas_call x1, Pallas kernels, body(): pl.pallas_call(functools.partial(kernel, n, row_dev, width, capacity), ou...  67.6 us
    unnamed x1, local copies, waits for them, and re-layouts  3.4 us

profile of v1, /device:TPU:1, one launch (start us, length us, event | category | flops | bytes accessed | tf_op | source)
XLA Modules:
  0.0 71.0 jit_solution(8063485702616339778)
XLA Ops:
  0.0 67.6 %shard_map.73 = bf16[256,5120]{1,0:T(8,128)(2,1)} custom-call(bf16[256,5120]{1,0:T(8,128)(2,1)} %bitcast.7, bf16[32,4096]{1,0:T(8,128)(2,1)} %amp_hbm.1, s32[4,80]{1,0:T(4,128)} %mask_ref.1, s32[1,4]{1,0:T(1,128)} %bitcast.8, s32[1,32]{1,0:T(1,128)} %bitcast.9, s32[1,32]{1,0:T(1,128)} %bitcast.10, s32[1,32]{1,0:T(1,128)} %bitcast.11), custom_call_target="tpu_custom_call" | custom-call | tf_op jit(solution)/shard_map/pallas_call | solution.py:247
  67.6 3.4 %copy.9 = bf16[4,64,5120]{2,1,0:T(8,128)(2,1)} copy(bf16[4,64,5120]{2,1,0:T(8,128)(2,1)} %bitcast.6) | data formatting | bytes 5242880

commit v2 on v1

--- a/solution.py
+++ b/solution.py
@@ -8,17 +8,18 @@
 from jax.sharding import PartitionSpec as P
 
 MESH = pl.DeviceIdType.MESH
-CHUNK = 512
-EARLY = 2
+CHUNK = 256
+EARLY = 4
+VMEM_LIMIT = 59 * 1024 * 1024
 
 
 def kernel(
     n, row_dev, width, capacity,
     panel_hbm, amp_hbm, mask_ref, rank_ref, owner_ref, row_ref, block_ref,
-    out_hbm,
-    gathered, amp, outbox, inbox, code_out, code_in, cells_s, block_f32, block_bf, staged,
+    out_ref,
+    gathered, amp, outbox, inbox, code_out, code_in, cells_s, block_f32, block_bf,
     load_sem, amp_sem, far_send, far_recv, mate_send, mate_recv, fwd_send, fwd_recv,
-    box_send, box_recv, code_send, code_recv, out_sem,
+    box_send, box_recv, code_send, code_recv,
 ):
     me = lax.axis_index("occ")
     ranks_of_chips = n // 2
@@ -82,21 +83,20 @@
             device_id={"occ": target}, device_id_type=MESH,
         )
 
-    @pl.loop(0, chunks)
-    def _(k):
-        load(k).start()
-
-    fetch_amp = pltpu.make_async_copy(amp_hbm, amp, amp_sem)
-    fetch_amp.start()
-
     barrier = pltpu.get_barrier_semaphore()
     for d in range(1, n):
         pl.semaphore_signal(barrier, inc=1, device_id={"occ": peer(d)}, device_id_type=MESH)
-    pl.semaphore_wait(barrier, n - 1)
+
+    @pl.loop(0, chunks)
+    def _(k):
+        load(k).start()
+
+    fetch_amp = pltpu.make_async_copy(amp_hbm, amp, amp_sem)
+    fetch_amp.start()
 
     col_tiles = mask_ref.shape[1]
 
-    def send_chunk(k):
+    def mask_chunk(k):
         tile_of = (k * CHUNK + lax.broadcasted_iota(jnp.int32, (col_tiles, CHUNK), 1)) // width
         spread = (tile_of == lax.broadcasted_iota(jnp.int32, (col_tiles, CHUNK), 0))
         kept = jnp.dot(
@@ -108,14 +108,21 @@
         for b in range(local_blocks):
             rows = pl.ds(pl.multiple_of(me * depth + b * width, width), width)
             gathered[k, rows, :] = gathered[k, rows, :] * kept[b : b + 1, :]
+
+    def send_chunk(k):
         for d in range(1, ranks_of_chips):
             far(k, d).start()
         near(k).start()
 
     early = min(EARLY, chunks)
 
-    @pl.loop(0, early)
-    def _(k):
+    mask_chunk(0)
+    pl.semaphore_wait(barrier, n - 1)
+    send_chunk(0)
+
+    @pl.loop(1, early)
+    def _(k):
+        mask_chunk(k)
         send_chunk(k)
 
     owner = owner_ref[...]
@@ -148,6 +155,7 @@
 
     @pl.loop(early, chunks)
     def _(k):
+        mask_chunk(k)
         send_chunk(k)
 
     inbox[me] = outbox[me]
@@ -194,17 +202,13 @@
     for q in range(blocks // 2):
         block_bf[:, q * 128 : (q + 1) * 128] = block_f32[q].astype(jnp.bfloat16)
 
-    def store(k):
-        return pltpu.make_async_copy(staged.at[k], out_hbm.at[:, columns(k)], out_sem.at[k])
-
     def multiply(k):
         near(k).wait_recv()
         for d in range(1, ranks_of_chips):
             forward(k, d).wait_recv()
-        staged[k] = jnp.dot(
+        out_ref[k] = jnp.dot(
             block_bf[...], gathered[k], preferred_element_type=jnp.float32
         ).astype(jnp.bfloat16)
-        store(k).start()
 
     def pass_on(k):
         for d in range(1, ranks_of_chips):
@@ -226,6 +230,21 @@
         for d in range(1, ranks_of_chips):
             far(k, d).wait_send()
             forward(k, d).wait_send()
+
+
+def write_kernel(held, out_hbm, out_sem):
+    chunks = held.shape[0]
+
+    def store(k):
+        place = pl.ds(pl.multiple_of(k * CHUNK, CHUNK), CHUNK)
+        return pltpu.make_async_copy(held.at[k], out_hbm.at[:, place], out_sem.at[k])
+
+    @pl.loop(0, chunks)
+    def _(k):
+        store(k).start()
+
+    @pl.loop(0, chunks)
+    def _(k):
         store(k).wait()
 
 
@@ -246,9 +265,9 @@
     dma = pltpu.SemaphoreType.DMA
     out = pl.pallas_call(
         functools.partial(kernel, n, row_dev, width, capacity),
-        out_shape=jax.ShapeDtypeStruct((row_dev * width, cols), jnp.bfloat16),
+        out_shape=pltpu.VMEM((chunks, row_dev * width, CHUNK), jnp.bfloat16),
         in_specs=[whole, whole] + [vmem] * 5,
-        out_specs=whole,
+        out_specs=vmem,
         scratch_shapes=[
             pltpu.VMEM((chunks, blocks * width, CHUNK), jnp.bfloat16),
             pltpu.VMEM((tiles, flat), jnp.bfloat16),
@@ -259,22 +278,26 @@
             pltpu.VMEM((flat // 128 * cells, 128), jnp.float32),
             pltpu.VMEM((blocks // 2, row_dev * width, 128), jnp.float32),
             pltpu.VMEM((row_dev * width, blocks * width), jnp.bfloat16),
-            pltpu.VMEM((chunks, row_dev * width, CHUNK), jnp.bfloat16),
             dma((chunks,)), dma,
             dma((chips - 1, chunks)), dma((chips - 1, chunks)),
             dma((chunks,)), dma((chunks,)),
             dma((chips - 1, chunks)), dma((chips - 1, chunks)),
             dma((others,)), dma((others,)), dma((others,)), dma((others,)),
-            dma((chunks,)),
         ],
         compiler_params=pltpu.CompilerParams(
-            collective_id=0, has_side_effects=True, vmem_limit_bytes=56 * 1024 * 1024
+            collective_id=0, has_side_effects=True, vmem_limit_bytes=VMEM_LIMIT
         ),
     )(
         panels.reshape(depth, cols), amplitudes, tile_mask, ranks[None], tile_owner[None],
         tile_row[None], tile_block[None],
     )
-    return out.reshape(row_dev, width, cols)
+    return pl.pallas_call(
+        write_kernel,
+        out_shape=jax.ShapeDtypeStruct((row_dev * width, cols), jnp.bfloat16),
+        in_specs=[vmem],
+        out_specs=whole,
+        scratch_shapes=[dma((chunks,))],
+    )(out).reshape(row_dev, width, cols)
 
 
 def solution(mesh):

time: 71.2 us -> 72.3 us (1.015)
  Pallas kernels: 67.6 us -> 70.6 us
  local copies, waits for them, and re-layouts: 3.4 us -> 1.51 us
    pallas_call x0 -> x1, Pallas kernels: none -> 3.38 us  [body(): pl.pallas_call(write_kernel, out_shape=jax.ShapeDtypeStruct((row_dev * wi...]
    unnamed x1 -> x2, local copies, waits for them, and re-layouts: 3.4 us -> 1.51 us
where the time goes in v2:
time: 72.3 us; the launch traced here: 72.1 us
  Pallas kernels  70.6 us (98%)
  local copies, waits for them, and re-layouts  1.51 us (2%)
    pallas_call x1, Pallas kernels, body(): pl.pallas_call(functools.partial(kernel, n, row_dev, width, capacity), ou...  67.2 us
    pallas_call x1, Pallas kernels, body(): pl.pallas_call(write_kernel, out_shape=jax.ShapeDtypeStruct((row_dev * wi...  3.38 us
    unnamed x2, local copies, waits for them, and re-layouts  1.51 us

profile of v2, /device:TPU:1, one launch (start us, length us, event | category | flops | bytes accessed | tf_op | source)
XLA Modules:
  0.0 72.1 jit_solution(7379640711168418488)
XLA Ops:
  0.0 67.2 %shard_map.73.held = bf16[20,256,256]{2,1,0:T(8,128)(2,1)S(1)} custom-call(bf16[256,5120]{1,0:T(8,128)(2,1)} %bitcast.6, bf16[32,4096]{1,0:T(8,128)(2,1)} %amp_hbm.1, s32[4,80]{1,0:T(4,128)} %mask_ref.1, s32[1,4]{1,0:T(1,128)} %bitcast.7, s32[1,32]{1,0:T(1,128)} %bitcast.8, s32[1,32]{1,0:T(1,128)} %bitcast.9, s32[1,32]{1,0:T(1,128)} %bitcast.10), custom_call_target="tpu_custom_call" | custom-call | tf_op jit(solution)/shard_map/pallas_call | solution.py:266
  67.2 0.0 copy-start
  67.2 1.5 %copy-done = bf16[20,256,256]{2,1,0:T(8,128)(2,1)} copy-done((bf16[20,256,256]{2,1,0:T(8,128)(2,1)}, bf16[20,256,256]{2,1,0:T(8,128)(2,1)S(1)}, u32[]{:S(2)}) %copy-start) | copy-done | bytes 2621464
  68.7 3.4 %shard_map.74 = bf16[256,5120]{1,0:T(8,128)(2,1)} custom-call(bf16[20,256,256]{2,1,0:T(8,128)(2,1)} %copy-done), custom_call_target="tpu_custom_call" | custom-call | tf_op jit(solution)/shard_map/pallas_call | solution.py:294
Async XLA Ops:
  67.2 1.5 %copy-start = (bf16[20,256,256]{2,1,0:T(8,128)(2,1)}, bf16[20,256,256]{2,1,0:T(8,128)(2,1)S(1)}, u32[]{:S(2)}) copy-start(bf16[20,256,256]{2,1,0:T(8,128)(2,1)S(1)} %shard_map.73.held) | copy-start | bytes 7864324

commit v3 on v2

--- a/solution.py
+++ b/solution.py
@@ -10,14 +10,16 @@
 MESH = pl.DeviceIdType.MESH
 CHUNK = 256
 EARLY = 4
+PARTS = 4
 VMEM_LIMIT = 59 * 1024 * 1024
 
 
 def kernel(
     n, row_dev, width, capacity,
-    panel_hbm, amp_hbm, mask_ref, rank_ref, owner_ref, row_ref, block_ref,
+    panel_hbm, amp_hbm, mask_hbm, rank_hbm, owner_hbm, row_hbm, block_hbm,
     out_ref,
     gathered, amp, outbox, inbox, code_out, code_in, cells_s, block_f32, block_bf,
+    mask_ref, rank_ref, owner_ref, row_ref, block_ref, small_sem,
     load_sem, amp_sem, far_send, far_recv, mate_send, mate_recv, fwd_send, fwd_recv,
     box_send, box_recv, code_send, code_recv,
 ):
@@ -87,7 +89,18 @@
     for d in range(1, n):
         pl.semaphore_signal(barrier, inc=1, device_id={"occ": peer(d)}, device_id_type=MESH)
 
-    @pl.loop(0, chunks)
+    small = [
+        pltpu.make_async_copy(source, target, small_sem.at[i])
+        for i, (source, target) in enumerate((
+            (mask_hbm, mask_ref), (rank_hbm, rank_ref), (owner_hbm, owner_ref),
+            (row_hbm, row_ref), (block_hbm, block_ref),
+        ))
+    ]
+    load(0).start()
+    for copy in small:
+        copy.start()
+
+    @pl.loop(1, chunks)
     def _(k):
         load(k).start()
 
@@ -116,6 +129,8 @@
 
     early = min(EARLY, chunks)
 
+    for copy in small:
+        copy.wait()
     mask_chunk(0)
     pl.semaphore_wait(barrier, n - 1)
     send_chunk(0)
@@ -206,7 +221,7 @@
         near(k).wait_recv()
         for d in range(1, ranks_of_chips):
             forward(k, d).wait_recv()
-        out_ref[k] = jnp.dot(
+        out_ref[:, columns(k)] = jnp.dot(
             block_bf[...], gathered[k], preferred_element_type=jnp.float32
         ).astype(jnp.bfloat16)
 
@@ -233,18 +248,16 @@
 
 
 def write_kernel(held, out_hbm, out_sem):
-    chunks = held.shape[0]
+    parts = out_sem.shape[0]
+    rows = held.shape[0] // parts
 
     def store(k):
-        place = pl.ds(pl.multiple_of(k * CHUNK, CHUNK), CHUNK)
-        return pltpu.make_async_copy(held.at[k], out_hbm.at[:, place], out_sem.at[k])
-
-    @pl.loop(0, chunks)
-    def _(k):
+        place = pl.ds(k * rows, rows)
+        return pltpu.make_async_copy(held.at[place, :], out_hbm.at[place, :], out_sem.at[k])
+
+    for k in range(parts):
         store(k).start()
-
-    @pl.loop(0, chunks)
-    def _(k):
+    for k in range(parts):
         store(k).wait()
 
 
@@ -265,8 +278,8 @@
     dma = pltpu.SemaphoreType.DMA
     out = pl.pallas_call(
         functools.partial(kernel, n, row_dev, width, capacity),
-        out_shape=pltpu.VMEM((chunks, row_dev * width, CHUNK), jnp.bfloat16),
-        in_specs=[whole, whole] + [vmem] * 5,
+        out_shape=pltpu.VMEM((row_dev * width, cols), jnp.bfloat16),
+        in_specs=[whole] * 7,
         out_specs=vmem,
         scratch_shapes=[
             pltpu.VMEM((chunks, blocks * width, CHUNK), jnp.bfloat16),
@@ -278,6 +291,12 @@
             pltpu.VMEM((flat // 128 * cells, 128), jnp.float32),
             pltpu.VMEM((blocks // 2, row_dev * width, 128), jnp.float32),
             pltpu.VMEM((row_dev * width, blocks * width), jnp.bfloat16),
+            pltpu.VMEM((local_blocks, cols // width), jnp.int32),
+            pltpu.VMEM((1, row_dev), jnp.int32),
+            pltpu.VMEM((1, tiles), jnp.int32),
+            pltpu.VMEM((1, tiles), jnp.int32),
+            pltpu.VMEM((1, tiles), jnp.int32),
+            dma((5,)),
             dma((chunks,)), dma,
             dma((chips - 1, chunks)), dma((chips - 1, chunks)),
             dma((chunks,)), dma((chunks,)),
@@ -296,7 +315,8 @@
         out_shape=jax.ShapeDtypeStruct((row_dev * width, cols), jnp.bfloat16),
         in_specs=[vmem],
         out_specs=whole,
-        scratch_shapes=[dma((chunks,))],
+        scratch_shapes=[dma((PARTS,))],
+        compiler_params=pltpu.CompilerParams(vmem_limit_bytes=1024 * 1024),
     )(out).reshape(row_dev, width, cols)
 
 

time: 72.3 us -> 68.3 us (0.945)
  Pallas kernels: 70.6 us -> 68.1 us
  local copies, waits for them, and re-layouts: 1.51 us -> 0 us
    pallas_call x1, Pallas kernels: 3.38 us -> 1.52 us  [body(): pl.pallas_call(write_kernel, out_shape=jax.ShapeDtypeStruct((row_dev * wi...]
    unnamed x2 -> x0, local copies, waits for them, and re-layouts: 1.51 us -> none
where the time goes in v3:
time: 68.3 us; the launch traced here: 68.1 us
  Pallas kernels  68.1 us (100%)
    pallas_call x1, Pallas kernels, body(): pl.pallas_call(functools.partial(kernel, n, row_dev, width, capacity), ou...  66.6 us
    pallas_call x1, Pallas kernels, body(): pl.pallas_call(write_kernel, out_shape=jax.ShapeDtypeStruct((row_dev * wi...  1.52 us

profile of v3, /device:TPU:1, one launch (start us, length us, event | category | flops | bytes accessed | tf_op | source)
XLA Modules:
  0.0 68.1 jit_solution(5189700787900392852)
XLA Ops:
  0.0 66.6 %shard_map.73.held = bf16[256,5120]{1,0:T(8,128)(2,1)S(1)} custom-call(bf16[256,5120]{1,0:T(8,128)(2,1)} %bitcast.6, bf16[32,4096]{1,0:T(8,128)(2,1)} %amp_hbm.1, s32[4,80]{1,0:T(4,128)} %mask_hbm.1, s32[1,4]{1,0:T(1,128)} %bitcast.7, s32[1,32]{1,0:T(1,128)} %bitcast.8, s32[1,32]{1,0:T(1,128)} %bitcast.9, s32[1,32]{1,0:T(1,128)} %bitcast.10), custom_call_target="tpu_custom_call" | custom-call | tf_op jit(solution)/shard_map/pallas_call | solution.py:279
  66.6 1.5 %shard_map.74 = bf16[256,5120]{1,0:T(8,128)(2,1)} custom-call(bf16[256,5120]{1,0:T(8,128)(2,1)S(1)} %shard_map.73.held), custom_call_target="tpu_custom_call" | custom-call | tf_op jit(solution)/shard_map/pallas_call | solution.py:313

commit v4 on v3

--- a/solution.py
+++ b/solution.py
@@ -8,8 +8,8 @@
 from jax.sharding import PartitionSpec as P
 
 MESH = pl.DeviceIdType.MESH
-CHUNK = 256
-EARLY = 4
+CHUNK = 512
+EARLY = 2
 PARTS = 4
 VMEM_LIMIT = 59 * 1024 * 1024
 

time: 68.3 us -> 67.9 us (level)
  no operation moved by 1% of the time
where the time goes in v4:
time: 67.9 us; the launch traced here: 67.8 us
  Pallas kernels  67.8 us (100%)
    pallas_call x1, Pallas kernels, body(): pl.pallas_call(functools.partial(kernel, n, row_dev, width, capacity), ou...  66.2 us
    pallas_call x1, Pallas kernels, body(): pl.pallas_call(write_kernel, out_shape=jax.ShapeDtypeStruct((row_dev * wi...  1.52 us

profile of v4, /device:TPU:1, one launch (start us, length us, event | category | flops | bytes accessed | tf_op | source)
XLA Modules:
  0.0 67.8 jit_solution(2991469775967143216)
XLA Ops:
  0.0 66.2 %shard_map.73.held = bf16[256,5120]{1,0:T(8,128)(2,1)S(1)} custom-call(bf16[256,5120]{1,0:T(8,128)(2,1)} %bitcast.6, bf16[32,4096]{1,0:T(8,128)(2,1)} %amp_hbm.1, s32[4,80]{1,0:T(4,128)} %mask_hbm.1, s32[1,4]{1,0:T(1,128)} %bitcast.7, s32[1,32]{1,0:T(1,128)} %bitcast.8, s32[1,32]{1,0:T(1,128)} %bitcast.9, s32[1,32]{1,0:T(1,128)} %bitcast.10), custom_call_target="tpu_custom_call" | custom-call | tf_op jit(solution)/shard_map/pallas_call | solution.py:279
  66.3 1.5 %shard_map.74 = bf16[256,5120]{1,0:T(8,128)(2,1)} custom-call(bf16[256,5120]{1,0:T(8,128)(2,1)S(1)} %shard_map.73.held), custom_call_target="tpu_custom_call" | custom-call | tf_op jit(solution)/shard_map/pallas_call | solution.py:313

commit v5 on v4

--- a/solution.py
+++ b/solution.py
@@ -51,7 +51,7 @@
         return pltpu.make_async_remote_copy(
             src_ref=slot(k, me), dst_ref=slot(k, me),
             send_sem=far_send.at[d - 1, k], recv_sem=far_recv.at[d - 1, k],
-            device_id={"occ": peer(2 * d)}, device_id_type=MESH,
+            device_id={"occ": lax.rem(mate + 2 * d, n)}, device_id_type=MESH,
         )
 
     def near(k):
@@ -62,7 +62,7 @@
         )
 
     def forward(k, d):
-        source = peer(n - 2 * d)
+        source = lax.rem(mate + n - 2 * d, n)
         return pltpu.make_async_remote_copy(
             src_ref=slot(k, source), dst_ref=slot(k, source),
             send_sem=fwd_send.at[d - 1, k], recv_sem=fwd_recv.at[d - 1, k],

time: 67.9 us -> 67.7 us (level)
  Pallas kernels: 67.8 us -> 66.9 us
    pallas_call x1, Pallas kernels: 66.2 us -> 65.4 us  [body(): pl.pallas_call(functools.partial(kernel, n, row_dev, width, capacity), ou...]
where the time goes in v5:
time: 67.7 us; the launch traced here: 66.9 us
  Pallas kernels  66.9 us (99%)
    pallas_call x1, Pallas kernels, body(): pl.pallas_call(functools.partial(kernel, n, row_dev, width, capacity), ou...  65.4 us
    pallas_call x1, Pallas kernels, body(): pl.pallas_call(write_kernel, out_shape=jax.ShapeDtypeStruct((row_dev * wi...  1.52 us

profile of v5, /device:TPU:1, one launch (start us, length us, event | category | flops | bytes accessed | tf_op | source)
XLA Modules:
  0.0 66.9 jit_solution(3771387290334866099)
XLA Ops:
  0.0 65.4 %shard_map.73.held = bf16[256,5120]{1,0:T(8,128)(2,1)S(1)} custom-call(bf16[256,5120]{1,0:T(8,128)(2,1)} %bitcast.6, bf16[32,4096]{1,0:T(8,128)(2,1)} %amp_hbm.1, s32[4,80]{1,0:T(4,128)} %mask_hbm.1, s32[1,4]{1,0:T(1,128)} %bitcast.7, s32[1,32]{1,0:T(1,128)} %bitcast.8, s32[1,32]{1,0:T(1,128)} %bitcast.9, s32[1,32]{1,0:T(1,128)} %bitcast.10), custom_call_target="tpu_custom_call" | custom-call | tf_op jit(solution)/shard_map/pallas_call | solution.py:279
  65.4 1.5 %shard_map.74 = bf16[256,5120]{1,0:T(8,128)(2,1)} custom-call(bf16[256,5120]{1,0:T(8,128)(2,1)S(1)} %shard_map.73.held), custom_call_target="tpu_custom_call" | custom-call | tf_op jit(solution)/shard_map/pallas_call | solution.py:313
